TPU v7x, 512 devices: a whole 4x8x8 slice. The times are simulated.
512 devices in a mesh: leaf: 32 (over y, x), row: 8 (over z), col: 2 (over core).
Axes of the slice: x: 4, y: 8, z: 8, core: 2. Of those that a mesh axis runs over, the one named last changes fastest.
Arguments:
- leaf_update: float32 [32, 512, 512], P('leaf', 'row', 'col'), as said below
- leaf_rhs: float32 [32, 512, 256], P('leaf', 'row', 'col'), may hold values from -6 to 6
- child_rows: int32 [31, 2, 512], replicated, may hold values from 0 to 1023, as said below
- separator_coef: float32 [31, 512], replicated, may hold values from 0.5 to 4
Outputs:
- final_update: float32 [512, 512], P('row', 'col')
- final_rhs: float32 [512, 256], P('row', 'col')
- separator_solutions: float32 [32, 512, 256], P('leaf', 'row', 'col')
Inputs may be any that keep to these rules, and one draw needn't show every extreme that they name: Each child_rows[f, c] lists 512 distinct rows of the front. Each leaf_update[i] is symmetric positive definite.
All inputs are finite; a program needn't handle non-finite values.
Results may differ from a plain program's by a relative error of at most 0.00017.
Values sent between devices are 32-bit elements; how exact they have to be, the bound alone decides.
A program may use at most 128 MiB of HBM per device.

v0:
```python
import jax
import jax.numpy as jnp
from jax import lax
from jax.sharding import PartitionSpec as P


def from_partner(block, axis, apart):
    count = lax.axis_size(axis)
    route = []
    for low in range(count):
        high = low | 1 << apart
        if high != low and high < count:
            route += [(low, high), (high, low)]
    return lax.ppermute(block, axis, route)


def stencil_block(sep_coefs):
    positions = jnp.arange(sep_coefs.shape[0], dtype=jnp.int32)
    distance = positions[:, None] - positions[None, :]
    return jnp.where(
        distance == 0, sep_coefs[:, None] + 2.0, jnp.where(jnp.abs(distance) == 1, -1.0, 0.0)
    )


def matmul_high(left, right):
    return jnp.dot(left, right, precision=lax.Precision.HIGHEST)


def factor_inverse(matrix):
    order = matrix.shape[0]
    if order <= 32:
        lower_factor = jnp.linalg.cholesky(matrix)
        identity = jnp.eye(order, dtype=matrix.dtype)
        return jax.scipy.linalg.solve_triangular(lower_factor, identity, lower=True)
    half = order // 2
    inv_top = factor_inverse(matrix[:half, :half])
    lower_left = matmul_high(matrix[half:, :half], inv_top.T)
    schur_part = matrix[half:, half:] - matmul_high(lower_left, lower_left.T)
    inv_bottom = factor_inverse(schur_part)
    inv_left = -matmul_high(inv_bottom, matmul_high(lower_left, inv_top))
    upper_rows = jnp.concatenate([inv_top, jnp.zeros((half, order - half), matrix.dtype)], axis=1)
    lower_rows = jnp.concatenate([inv_left, inv_bottom], axis=1)
    return jnp.concatenate([upper_rows, lower_rows], axis=0)


def inverse_map(mapping, front_size):
    sources = jnp.arange(mapping.shape[0], dtype=jnp.int32)
    return jnp.full((front_size,), -1, jnp.int32).at[mapping].set(sources)


def spread_rows(full_rows, inverse, parent_rows):
    source = inverse[parent_rows]
    present = source >= 0
    picked = jnp.take(full_rows, jnp.maximum(source, 0), axis=0)
    return jnp.where(present[:, None], picked, 0.0)


def spread_block(full_matrix, inverse, parent_rows, parent_cols):
    src_rows = inverse[parent_rows]
    src_cols = inverse[parent_cols]
    picked = jnp.take(
        jnp.take(full_matrix, jnp.maximum(src_rows, 0), axis=0), jnp.maximum(src_cols, 0), axis=1
    )
    present = (src_rows >= 0)[:, None] & (src_cols >= 0)[None, :]
    return jnp.where(present, picked, 0.0)


def per_device(leaf_update, leaf_rhs, child_rows, separator_coef):
    update_blk = leaf_update[0]
    rhs_blk = leaf_rhs[0]
    leaf_count = lax.axis_size("leaf")
    row_count = lax.axis_size("row")
    col_count = lax.axis_size("col")
    levels = leaf_count.bit_length() - 1
    leaf_index = lax.axis_index("leaf")
    row_index = lax.axis_index("row")
    col_index = lax.axis_index("col")
    row_block, col_block = update_blk.shape
    rhs_cols = rhs_blk.shape[1]
    update_size = row_block * row_count
    sep_size = separator_coef.shape[1]
    front_size = sep_size + update_size
    sep_rows = jnp.arange(sep_size, dtype=jnp.int32)
    own_rows = sep_size + row_index * row_block + jnp.arange(row_block, dtype=jnp.int32)
    own_cols = sep_size + col_index * col_block + jnp.arange(col_block, dtype=jnp.int32)
    sep_share = sep_size // row_count
    kept_rows = jnp.zeros((sep_share, rhs_cols), jnp.float32)
    offset = 0
    for level_no in range(1, levels + 1):
        bit_no = level_no - 1
        other_upd, other_rhs = from_partner((update_blk, rhs_blk), "leaf", bit_no)
        blocks = lax.all_gather(
            jnp.stack([update_blk, other_upd])[:, None], ("row", "col"), axis=1, tiled=True
        )
        whole_rhs = lax.all_gather(jnp.stack([rhs_blk, other_rhs]), "row", axis=1, tiled=True)
        whole_upd = (
            blocks.reshape(2, row_count, col_count, row_block, col_block)
            .transpose(0, 1, 3, 2, 4)
            .reshape(2, update_size, update_size)
        )
        own_upd, partner_upd = (whole_upd[0], whole_upd[1])
        own_rhs, partner_rhs = (whole_rhs[0], whole_rhs[1])
        out_rows, out_cols = (own_rows, own_cols)
        upper_half = leaf_index >> bit_no & 1 == 1
        first_upd = jnp.where(upper_half, partner_upd, own_upd)
        second_upd = jnp.where(upper_half, own_upd, partner_upd)
        first_rhs = jnp.where(upper_half, partner_rhs, own_rhs)
        second_rhs = jnp.where(upper_half, own_rhs, partner_rhs)
        front_id = offset + (leaf_index >> level_no)
        mapping = lax.dynamic_index_in_dim(child_rows, front_id, 0, keepdims=False)
        sep_coefs = lax.dynamic_index_in_dim(separator_coef, front_id, 0, keepdims=False)
        inv_first = inverse_map(mapping[0], front_size)
        inv_second = inverse_map(mapping[1], front_size)

        def assemble(parent_rows, parent_cols):
            return spread_block(first_upd, inv_first, parent_rows, parent_cols) + spread_block(
                second_upd, inv_second, parent_rows, parent_cols
            )

        diag_block = stencil_block(sep_coefs) + assemble(sep_rows, sep_rows)
        factor_inv = factor_inverse(diag_block)
        panel_rows = matmul_high(factor_inv, assemble(out_rows, sep_rows).T)
        panel_cols = matmul_high(factor_inv, assemble(out_cols, sep_rows).T)
        update_blk = assemble(out_rows, out_cols) - matmul_high(panel_rows.T, panel_cols)
        rhs_sep = spread_rows(first_rhs, inv_first, sep_rows) + spread_rows(
            second_rhs, inv_second, sep_rows
        )
        rhs_own = spread_rows(first_rhs, inv_first, out_rows) + spread_rows(
            second_rhs, inv_second, out_rows
        )
        solved = matmul_high(factor_inv, rhs_sep)
        rhs_blk = rhs_own - matmul_high(panel_rows.T, solved)
        store_here = leaf_index & (1 << level_no) - 1 == 1 << bit_no
        if level_no == levels:
            store_here = store_here | (leaf_index & (1 << bit_no) - 1 == 0)
        kept_rows = jnp.where(
            store_here,
            lax.dynamic_slice_in_dim(solved, row_index * sep_share, sep_share, 0),
            kept_rows,
        )
        offset += leaf_count >> level_no
    return (update_blk, rhs_blk, kept_rows[None])


def solution(mesh):
    in_specs = (P("leaf", "row", "col"), P("leaf", "row", "col"), P(), P())
    out_specs = (P("row", "col"), P("row", "col"), P("leaf", "row", "col"))
    return jax.shard_map(
        per_device, mesh=mesh, in_specs=in_specs, out_specs=out_specs, check_vma=False
    )
```

profile of v0, /device:TPU:56, one launch (start us, length us, event | category | flops | bytes accessed | tf_op | source)
XLA Modules:
  0.0 1204.7 jit_solution(3808599444853935362)
XLA Ops:
  7.2 3.4 collective-permute-start
  10.6 3.0 collective-permute-done
  21.3 3.0 scatter_custom_fusion.5
  35.0 27.5 %all-gather.11.cloned.1.call-done = f32[2,1024,256]{2,1,0:T(8,128)} async-done(((f32[2,64,256]{2,1,0:T(8,128)}), f32[2,1024,256]{2,1,0:T(8,128)}) %all-gather.11.cloned.1.call-update) | async-done | bytes 2097168 | tf_op jit(solution)/shard_map/all_gather | solution.py:92
  62.5 3.2 copy.566
  98.4 2.9 cholesky.1225
  129.8 2.9 cholesky.1269
  145.3 2.9 cholesky.1291
  177.8 3.1 cholesky.1335
  193.8 2.9 cholesky.1357
  224.9 4.9 collective-permute-start.1
  259.6 15.1 %all-gather.13.cloned.1.call-done = f32[2,1024,256]{2,1,0:T(8,128)} async-done(((f32[2,64,256]{2,1,0:T(8,128)}), f32[2,1024,256]{2,1,0:T(8,128)}) %all-gather.13.cloned.1.call-update) | async-done | bytes 2097168 | tf_op jit(solution)/shard_map/all_gather | solution.py:92
  310.6 2.9 cholesky.1401
  342.1 2.9 cholesky.1445
  357.7 2.9 cholesky.1467
  375.4 2.9 cholesky.1489
  391.0 3.1 cholesky.1511
  407.1 2.9 cholesky.1533
  438.1 3.4 collective-permute-start.2
  445.0 3.4 collective-permute-start.5
  482.3 4.1 all-gather.15.cloned.1.call-done
  522.7 2.9 cholesky.1577
  554.7 2.9 cholesky.1621
  604.1 3.1 cholesky.1687
  620.4 2.9 cholesky.1709
  651.4 4.2 collective-permute-start.3
  656.2 3.6 collective-permute-done.3
  674.3 26.1 %all_gather.35 = f32[2,512,128]{2,1,0:T(8,128)S(1)} all-gather(f32[2,64,128]{2,1,0:T(8,128)S(1)} %pad_maximum_fusion.5), channel_id=1, replica_groups=mesh['leaf'=32,'row'=8,'col'=2] {'row'}, dimensions={1}, use_global_device_ids=true | all-gather | bytes 589824 | tf_op jit(solution)/shard_map/all_gather | solution.py:95
  706.8 5.2 collective-permute-start.6
  747.3 2.9 cholesky.1753
  811.8 2.9 cholesky.1841
  827.4 3.3 cholesky.1863
  843.6 2.9 cholesky.1885
  874.3 5.0 collective-permute-start.4
  880.2 4.4 collective-permute-done.4
  885.2 26.0 %all_gather.36 = f32[2,512,128]{2,1,0:T(8,128)S(1)} all-gather(f32[2,64,128]{2,1,0:T(8,128)S(1)} %pad_maximum_fusion.6), channel_id=1, replica_groups=mesh['leaf'=32,'row'=8,'col'=2] {'row'}, dimensions={1}, use_global_device_ids=true | all-gather | bytes 589824 | tf_op jit(solution)/shard_map/all_gather | solution.py:95
  918.6 3.9 collective-permute-done.7
  922.4 25.7 %all_gather.37 = f32[2,512,128]{2,1,0:T(8,128)S(1)} all-gather(f32[2,64,128]{2,1,0:T(8,128)S(1)} %pad_maximum_fusion.7), channel_id=1, replica_groups=mesh['leaf'=32,'row'=8,'col'=2] {'row'}, dimensions={1}, use_global_device_ids=true | all-gather | bytes 589824 | tf_op jit(solution)/shard_map/all_gather | solution.py:95
  953.6 3.2 collective-permute-start.8
  956.8 3.5 collective-permute-done.8
  960.3 25.3 %all_gather.38 = f32[2,512,128]{2,1,0:T(8,128)S(1)} all-gather(f32[2,64,128]{2,1,0:T(8,128)S(1)} %pad_maximum_fusion.8), channel_id=1, replica_groups=mesh['leaf'=32,'row'=8,'col'=2] {'row'}, dimensions={1}, use_global_device_ids=true | all-gather | bytes 589824 | tf_op jit(solution)/shard_map/all_gather | solution.py:95
  991.2 5.0 collective-permute-start.9
  996.3 5.0 collective-permute-done.9
  1001.3 25.2 %all_gather.39 = f32[2,512,128]{2,1,0:T(8,128)S(1)} all-gather(f32[2,64,128]{2,1,0:T(8,128)S(1)} %pad_maximum_fusion.9), channel_id=1, replica_groups=mesh['leaf'=32,'row'=8,'col'=2] {'row'}, dimensions={1}, use_global_device_ids=true | all-gather | bytes 589824 | tf_op jit(solution)/shard_map/all_gather | solution.py:95
  1099.1 2.9 cholesky.1973
  1114.6 2.9 cholesky.1995
  1147.1 3.1 cholesky.2039
  1163.1 2.9 cholesky.2061
  (1930 shorter events, 870.5 us)
Async XLA Ops:
  7.2 55.3 %all-gather.11.cloned.1.call-start = ((), (), s32[]{:S(2)}) async-start(), calls=%async_computation | async-start | bytes 2228224 | tf_op jit(solution)/shard_map/all_gather | solution.py:92
  7.2 6.4 collective-permute-start
  15.1 259.6 %all-gather.13.cloned.1.call-start = ((), (), s32[]{:S(2)}) async-start(), calls=%async_computation.1 | async-start | bytes 2228224 | tf_op jit(solution)/shard_map/all_gather | solution.py:92
  31.0 180.8 %copy-start.89 = (s32[1024]{0:T(1024)}, s32[1024]{0:T(1024)S(1)}, u32[]{:S(2)}) copy-start(s32[1024]{0:T(1024)S(1)} %pad_clamp_fusion.24) | copy-start | bytes 12292
  31.7 178.2 %copy-start.91 = (s32[1024]{0:T(1024)}, s32[1024]{0:T(1024)S(1)}, u32[]{:S(2)}) copy-start(s32[1024]{0:T(1024)S(1)} %pad_clamp_fusion.25) | copy-start | bytes 12292
  31.7 35.0 %copy-start.144 = (s32[1024]{0:T(1024)}, s32[1024]{0:T(1024)S(1)}, u32[]{:S(2)}) copy-start(s32[1024]{0:T(1024)S(1)} %pad_clamp_fusion.30) | copy-start | bytes 12292
  33.8 33.6 %copy-start.198 = (pred[64]{0:T(512)(128)(4,1)}, pred[64]{0:T(512)(128)(4,1)S(1)}, u32[]{:S(2)}) copy-start(pred[64]{0:T(512)(128)(4,1)S(1)} %get-tuple-element.167) | copy-start | bytes 196
  153.0 69.9 %copy-start.25 = (f32[256,256]{1,0:T(8,128)}, f32[256,256]{1,0:T(8,128)S(1)}, u32[]{:S(2)}) copy-start(f32[256,256]{1,0:T(8,128)S(1)} %select_maximum_fusion.9) | copy-start | bytes 786436
  154.5 54.8 %copy-start.24 = (f32[256,64]{1,0:T(8,128)S(1)}, f32[256,64]{1,0:T(8,128)}, u32[]{:S(2)}) copy-start(f32[256,64]{1,0:T(8,128)} %gather_fusion.33) | copy-start | bytes 196612
  162.2 47.3 %copy-start = (f32[256,512]{1,0:T(8,128)S(1)}, f32[256,512]{1,0:T(8,128)}, u32[]{:S(2)}) copy-start(f32[256,512]{1,0:T(8,128)} %gather_fusion.40) | copy-start | bytes 1572868
  162.2 47.3 %copy-start.226 = (pred[256]{0:T(512)(128)(4,1)S(1)}, pred[256]{0:T(512)(128)(4,1)}, u32[]{:S(2)}) copy-start(pred[256]{0:T(512)(128)(4,1)} %get-tuple-element.143) | copy-start | bytes 772
  224.9 7.7 collective-permute-start.1
  233.2 253.1 %all-gather.15.cloned.1.call-start = ((), (), s32[]{:S(2)}) async-start(), calls=%async_computation.2 | async-start | bytes 2228224 | tf_op jit(solution)/shard_map/all_gather | solution.py:92
  251.9 24.5 %copy-start.132 = (s32[256]{0:T(256)}, s32[256]{0:T(256)S(1)}, u32[]{:S(2)}) copy-start(s32[256]{0:T(256)S(1)} %gather_fusion.5) | copy-start | bytes 3076
  255.9 169.2 %copy-start.93 = (s32[1024]{0:T(1024)}, s32[1024]{0:T(1024)S(1)}, u32[]{:S(2)}) copy-start(s32[1024]{0:T(1024)S(1)} %pad_clamp_fusion.18) | copy-start | bytes 12292
  257.2 24.2 %copy-start.95 = (s32[1024]{0:T(1024)}, s32[1024]{0:T(1024)S(1)}, u32[]{:S(2)}) copy-start(s32[1024]{0:T(1024)S(1)} %pad_clamp_fusion.19) | copy-start | bytes 12292
  365.4 70.8 %copy-start.27 = (f32[256,256]{1,0:T(8,128)}, f32[256,256]{1,0:T(8,128)S(1)}, u32[]{:S(2)}) copy-start(f32[256,256]{1,0:T(8,128)S(1)} %select_maximum_fusion.8) | copy-start | bytes 786436
  367.6 55.0 %copy-start.18 = (f32[256,64]{1,0:T(8,128)S(1)}, f32[256,64]{1,0:T(8,128)}, u32[]{:S(2)}) copy-start(f32[256,64]{1,0:T(8,128)} %gather_fusion.45) | copy-start | bytes 196612
  375.0 47.8 %copy-start.1 = (f32[256,512]{1,0:T(8,128)S(1)}, f32[256,512]{1,0:T(8,128)}, u32[]{:S(2)}) copy-start(f32[256,512]{1,0:T(8,128)} %gather_fusion.54) | copy-start | bytes 1572868
  375.0 47.8 %copy-start.223 = (pred[256]{0:T(512)(128)(4,1)S(1)}, pred[256]{0:T(512)(128)(4,1)}, u32[]{:S(2)}) copy-start(pred[256]{0:T(512)(128)(4,1)} %get-tuple-element.82) | copy-start | bytes 772
  438.1 6.2 collective-permute-start.2
  444.9 267.1 %all-gather.17.cloned.1.call-start = ((), (), s32[]{:S(2)}) async-start(), calls=%async_computation.3 | async-start | bytes 2228224 | tf_op jit(solution)/shard_map/all_gather | solution.py:92
  445.0 228.6 %collective-permute-start.5 = (f32[64,128]{1,0:T(8,128)}, f32[64,128]{1,0:T(8,128)}, u32[]{:S(2)}, u32[]{:S(2)}) collective-permute-start(f32[64,128]{1,0:T(8,128)} %bitcast.331), channel_id=1, source_target_pairs={{0,16},{16,0},{32,48},{48,32},{64,80},{80,64},{96,112},{112,96},{1... | collective-permute-start | bytes 98312 | tf_op jit(solution)/shard_map/ppermute | solution.py:14
  452.7 27.1 %copy-start.128 = (s32[256]{0:T(256)}, s32[256]{0:T(256)S(1)}, u32[]{:S(2)}) copy-start(s32[256]{0:T(256)S(1)} %gather_fusion.1) | copy-start | bytes 3076
  455.0 26.0 %copy-start.116 = (s32[512]{0:T(512)}, s32[512]{0:T(512)S(1)}, u32[]{:S(2)}) copy-start(s32[512]{0:T(512)S(1)} %gather_fusion.28) | copy-start | bytes 6148
  578.3 71.3 %copy-start.29 = (f32[256,256]{1,0:T(8,128)}, f32[256,256]{1,0:T(8,128)S(1)}, u32[]{:S(2)}) copy-start(f32[256,256]{1,0:T(8,128)S(1)} %select_maximum_fusion.7) | copy-start | bytes 786436
  580.5 55.6 %copy-start.19 = (f32[256,64]{1,0:T(8,128)S(1)}, f32[256,64]{1,0:T(8,128)}, u32[]{:S(2)}) copy-start(f32[256,64]{1,0:T(8,128)} %gather_fusion.59) | copy-start | bytes 196612
  587.9 48.3 %copy-start.2 = (f32[256,512]{1,0:T(8,128)S(1)}, f32[256,512]{1,0:T(8,128)}, u32[]{:S(2)}) copy-start(f32[256,512]{1,0:T(8,128)} %gather_fusion.68) | copy-start | bytes 1572868
  587.9 48.3 %copy-start.219 = (pred[256]{0:T(512)(128)(4,1)S(1)}, pred[256]{0:T(512)(128)(4,1)}, u32[]{:S(2)}) copy-start(pred[256]{0:T(512)(128)(4,1)} %get-tuple-element.145) | copy-start | bytes 772
  651.4 8.5 collective-permute-start.3
  660.5 371.8 %all-gather.19.cloned.1.call-start = ((), (), s32[]{:S(2)}) async-start(), calls=%async_computation.4 | async-start | bytes 2228224 | tf_op jit(solution)/shard_map/all_gather | solution.py:92
  664.1 37.0 %copy-start.92 = (s32[1024]{0:T(1024)S(1)}, s32[1024]{0:T(1024)}, u32[]{:S(2)}) copy-start(s32[1024]{0:T(1024)} %copy-done.91) | copy-start | bytes 12292
  670.0 48.1 %copy-start.108 = (s32[1024]{0:T(1024)}, s32[1024]{0:T(1024)S(1)}, u32[]{:S(2)}) copy-start(s32[1024]{0:T(1024)S(1)} %pad_clamp_fusion.7) | copy-start | bytes 12292
  670.6 44.7 %copy-start.214 = (pred[64]{0:T(512)(128)(4,1)}, pred[64]{0:T(512)(128)(4,1)S(1)}, u32[]{:S(2)}) copy-start(pred[64]{0:T(512)(128)(4,1)S(1)} %get-tuple-element.155) | copy-start | bytes 196
  673.5 41.1 %copy-start.147 = (s32[1024]{0:T(1024)}, s32[1024]{0:T(1024)S(1)}, u32[]{:S(2)}) copy-start(s32[1024]{0:T(1024)S(1)} %pad_clamp_fusion.11) | copy-start | bytes 12292
  706.8 172.6 %collective-permute-start.6 = (f32[64,128]{1,0:T(8,128)}, f32[64,128]{1,0:T(8,128)}, u32[]{:S(2)}, u32[]{:S(2)}) collective-permute-start(f32[64,128]{1,0:T(8,128)} %convolution_subtract_fusion.44), channel_id=1, source_target_pairs={{0,32},{32,0},{16,48},{48,16},{64,96},{96,64},{80,112},{112,80},{1... | collective-permute-start | bytes 98312 | tf_op jit(solution)/shard_map/ppermute | solution.py:14
  811.4 47.8 %copy-start.3 = (f32[256,512]{1,0:T(8,128)S(1)}, f32[256,512]{1,0:T(8,128)}, u32[]{:S(2)}) copy-start(f32[256,512]{1,0:T(8,128)} %gather_fusion.82) | copy-start | bytes 1572868
  811.4 47.8 %copy-start.221 = (pred[256]{0:T(512)(128)(4,1)S(1)}, pred[256]{0:T(512)(128)(4,1)}, u32[]{:S(2)}) copy-start(pred[256]{0:T(512)(128)(4,1)} %get-tuple-element.74) | copy-start | bytes 772
  873.9 38.0 %copy-start.98 = (s32[1024]{0:T(1024)S(1)}, s32[1024]{0:T(1024)}, u32[]{:S(2)}) copy-start(s32[1024]{0:T(1024)} %copy-done.95) | copy-start | bytes 12292
  874.3 10.2 collective-permute-start.4
  916.3 31.9 %copy-start.15 = (f32[512,128]{1,0:T(8,128)}, f32[512,128]{1,0:T(8,128)S(1)}, u32[]{:S(2)}) copy-start(f32[512,128]{1,0:T(8,128)S(1)} %fusion.306) | copy-start | bytes 786436
  916.3 32.6 %copy-start.106 = (s32[1024]{0:T(1024)S(1)}, s32[1024]{0:T(1024)}, u32[]{:S(2)}) copy-start(s32[1024]{0:T(1024)} %copy-done.103) | copy-start | bytes 12292
  916.6 5.8 collective-permute-start.7
  953.3 32.4 %copy-start.16 = (f32[512,128]{1,0:T(8,128)}, f32[512,128]{1,0:T(8,128)S(1)}, u32[]{:S(2)}) copy-start(f32[512,128]{1,0:T(8,128)S(1)} %fusion.303) | copy-start | bytes 786436
  953.6 6.8 collective-permute-start.8
  991.2 10.1 collective-permute-start.9
  1131.1 47.6 %copy-start.4 = (f32[256,512]{1,0:T(8,128)S(1)}, f32[256,512]{1,0:T(8,128)}, u32[]{:S(2)}) copy-start(f32[256,512]{1,0:T(8,128)} %gather_fusion.96) | copy-start | bytes 1572868
  1131.1 47.6 %copy-start.217 = (pred[256]{0:T(512)(128)(4,1)S(1)}, pred[256]{0:T(512)(128)(4,1)}, u32[]{:S(2)}) copy-start(pred[256]{0:T(512)(128)(4,1)} %get-tuple-element.147) | copy-start | bytes 772
  (237 other events, 1089.9 us)
Sparse Core Ops, SparseCore 0:
  15.2 47.2 all-gather.10
  233.4 41.2 all-gather.12
  445.0 41.2 all-gather.14
  660.7 42.0 all-gather.16
  885.3 39.5 all-gather.18
where the time goes:
time: 1210 us; the launch traced here: 1200 us
  other arithmetic  596 us (49%)
  local copies, waits for them, and re-layouts  231 us (19%)
  blocking collectives  128 us (11%)
  matrix products  110 us (9%)
  waiting for transfers between devices  75.7 us (6%)
  starting transfers between devices  39.8 us (3%)
  between operations  23.6 us (2%)
    another operation x240, other arithmetic, factor_inverse(): lower_factor = jnp.linalg.cholesky(matrix)  291 us
    another operation x160, other arithmetic, factor_inverse(): return jax.scipy.linalg.solve_triangular(lower_factor, identity, lower=True)  247 us
    all_gather x5, blocking collectives, per_device(): lax.all_gather(jnp.stack([rhs_blk, other_rhs]), 'row', axis=1, tiled=True)  128 us
    dot_general x325, matrix products, matmul_high(): return jnp.dot(left, right, precision=lax.Precision.HIGHEST)  91 us
    gather x50, local copies, waits for them, and re-layouts, spread_block(): jnp.take(jnp.take(full_matrix, jnp.maximum(src_rows, 0), axis=0), jnp.max...  60.6 us
    all_gather x5, waiting for transfers between devices, per_device(): lax.all_gather(jnp.stack([update_blk, other_upd])[:, None], ('row', 'col'...  46.7 us
    gather x30, local copies, waits for them, and re-layouts, spread_block(): jnp.take(full_matrix, jnp.maximum(src_rows, 0), axis=0)  41.8 us
    ppermute x10, starting transfers between devices, from_partner(): return lax.ppermute(block, axis, route)  39.6 us
  transfers between devices with their start and end apart: 15, of which 11 were waited for; matrix products, arithmetic and copies ran while one was open for 37% of the time, Pallas kernels for 0%

commit v1 on v0

--- a/solution.py
+++ b/solution.py
@@ -92,7 +92,11 @@
         blocks = lax.all_gather(
             jnp.stack([update_blk, other_upd])[:, None], ("row", "col"), axis=1, tiled=True
         )
-        whole_rhs = lax.all_gather(jnp.stack([rhs_blk, other_rhs]), "row", axis=1, tiled=True)
+        own = jnp.stack([rhs_blk, other_rhs])
+        count_2 = lax.axis_size("row")
+        pieces = jnp.stack([own for _ in range(count_2)])
+        pieces = lax.all_to_all(pieces, "row", split_axis=0, concat_axis=0)
+        whole_rhs = jnp.concatenate(pieces, axis=1)
         whole_upd = (
             blocks.reshape(2, row_count, col_count, row_block, col_block)
             .transpose(0, 1, 3, 2, 4)

time: 1210 us -> 1160 us (0.959)
  blocking collectives: 128 us -> 0 us
  waiting for transfers between devices: 75.7 us -> 129 us
  starting transfers between devices: 39.8 us -> 63.7 us
    all_gather x5 -> x0, blocking collectives: 128 us -> none  [per_device(): lax.all_gather(jnp.stack([rhs_blk, other_rhs]), 'row', axis=1, tiled=True)]
    all_to_all x0 -> x5, waiting for transfers between devices: none -> 41.2 us  [per_device(): pieces = lax.all_to_all(pieces, 'row', split_axis=0, concat_axis=0)]
    all_to_all x0 -> x5, starting transfers between devices: none -> 23.2 us  [per_device(): pieces = lax.all_to_all(pieces, 'row', split_axis=0, concat_axis=0)]
    all_gather x5, waiting for transfers between devices: 46.7 us -> 60.6 us  [per_device(): lax.all_gather(jnp.stack([update_blk, other_upd])[:, None], ('row', 'col'...]
  transfers between devices with their start and end apart: 15 -> 20, of which waited for: 11 -> 15; matrix products, arithmetic and copies ran while one was open for 37% -> 39% of each run, Pallas kernels for 0% -> 0%
where the time goes in v1:
time: 1160 us; the launch traced here: 1150 us
  other arithmetic  592 us (51%)
  local copies, waits for them, and re-layouts  234 us (20%)
  waiting for transfers between devices  129 us (11%)
  matrix products  109 us (9%)
  starting transfers between devices  63.7 us (5%)
  between operations  23.5 us (2%)
    another operation x240, other arithmetic, factor_inverse(): lower_factor = jnp.linalg.cholesky(matrix)  290 us
    another operation x160, other arithmetic, factor_inverse(): return jax.scipy.linalg.solve_triangular(lower_factor, identity, lower=True)  245 us
    dot_general x325, matrix products, matmul_high(): return jnp.dot(left, right, precision=lax.Precision.HIGHEST)  90.4 us
    all_gather x5, waiting for transfers between devices, per_device(): lax.all_gather(jnp.stack([update_blk, other_upd])[:, None], ('row', 'col'...  60.6 us
    gather x50, local copies, waits for them, and re-layouts, spread_block(): jnp.take(jnp.take(full_matrix, jnp.maximum(src_rows, 0), axis=0), jnp.max...  60.6 us
    gather x30, local copies, waits for them, and re-layouts, spread_block(): jnp.take(full_matrix, jnp.maximum(src_rows, 0), axis=0)  41.8 us
    all_to_all x5, waiting for transfers between devices, per_device(): pieces = lax.all_to_all(pieces, 'row', split_axis=0, concat_axis=0)  41.2 us
    ppermute x10, starting transfers between devices, from_partner(): return lax.ppermute(block, axis, route)  40.2 us
  transfers between devices with their start and end apart: 20, of which 15 were waited for; matrix products, arithmetic and copies ran while one was open for 39% of the time, Pallas kernels for 0%

profile of v1, /device:TPU:56, one launch (start us, length us, event | category | flops | bytes accessed | tf_op | source)
XLA Modules:
  0.0 1151.3 jit_solution(4540124459350738485)
XLA Ops:
  7.2 3.4 collective-permute-start
  10.6 3.0 collective-permute-done
  35.2 27.3 %all-gather.11.cloned.1.call-done = f32[2,1024,256]{2,1,0:T(8,128)} async-done(((f32[2,64,256]{2,1,0:T(8,128)}), f32[2,1024,256]{2,1,0:T(8,128)}) %all-gather.11.cloned.1.call-update) | async-done | bytes 2097168 | tf_op jit(solution)/shard_map/all_gather | solution.py:92
  62.5 3.2 copy.795
  98.7 2.9 cholesky.1225
  130.2 2.9 cholesky.1269
  145.7 2.9 cholesky.1291
  178.1 3.1 cholesky.1335
  194.2 2.9 cholesky.1357
  225.0 4.9 collective-permute-start.1
  261.9 12.9 %all-gather.13.cloned.1.call-done = f32[2,1024,256]{2,1,0:T(8,128)} async-done(((f32[2,64,256]{2,1,0:T(8,128)}), f32[2,1024,256]{2,1,0:T(8,128)}) %all-gather.13.cloned.1.call-update) | async-done | bytes 2097168 | tf_op jit(solution)/shard_map/all_gather | solution.py:92
  311.2 2.9 cholesky.1401
  342.3 2.9 cholesky.1445
  357.7 2.9 cholesky.1467
  375.2 2.9 cholesky.1489
  390.6 3.1 cholesky.1511
  406.5 2.9 cholesky.1533
  437.1 3.4 collective-permute-start.2
  443.9 3.4 collective-permute-start.5
  465.0 20.4 %all-gather.15.cloned.1.call-done = f32[2,1024,256]{2,1,0:T(8,128)} async-done(((f32[2,64,256]{2,1,0:T(8,128)}), f32[2,1024,256]{2,1,0:T(8,128)}) %all-gather.15.cloned.1.call-update) | async-done | bytes 2097168 | tf_op jit(solution)/shard_map/all_gather | solution.py:92
  521.7 2.9 cholesky.1577
  552.8 2.9 cholesky.1621
  601.0 3.1 cholesky.1687
  616.8 2.9 cholesky.1709
  647.6 4.2 collective-permute-start.3
  653.5 4.2 all-to-all-start
  668.3 7.0 all-to-all-done
  681.1 4.9 collective-permute-start.6
  689.3 3.5 all-to-all-start.1
  701.3 8.3 all-to-all-done.1
  715.5 3.4 collective-permute-start.7
  722.2 4.1 all-to-all-start.2
  761.7 2.9 cholesky.1753
  809.2 2.9 cholesky.1819
  842.7 3.1 cholesky.1863
  889.9 4.3 collective-permute-start.4
  894.2 5.7 collective-permute-done.4
  907.1 3.3 collective-permute-start.8
  910.3 3.4 collective-permute-done.8
  914.6 7.5 all-to-all-start.3
  926.8 13.3 %all-to-all-done.3 = f32[8,2,64,128]{3,2,1,0:T(8,128)S(1)} async-done(((f32[8,2,64,128]{3,2,1,0:T(8,128)}), f32[8,2,64,128]{3,2,1,0:T(8,128)S(1)}, u32[]{:S(2)}, u32[]{:S(2)}) %all-to-all-start.3) | async-done | bytes 524320 | tf_op jit(solution)/shard_map/all_to_all | solution.py:98
  945.6 5.2 collective-permute-start.9
  950.8 4.5 collective-permute-done.9
  956.2 4.0 all-to-all-start.4
  960.8 12.7 %all-to-all-done.4 = f32[8,2,64,128]{3,2,1,0:T(8,128)S(1)} async-done(((f32[8,2,64,128]{3,2,1,0:T(8,128)}), f32[8,2,64,128]{3,2,1,0:T(8,128)S(1)}, u32[]{:S(2)}, u32[]{:S(2)}) %all-to-all-start.4) | async-done | bytes 524320 | tf_op jit(solution)/shard_map/all_to_all | solution.py:98
  1014.2 2.9 cholesky.1929
  1078.0 2.9 cholesky.2017
  1093.6 3.1 cholesky.2039
  (1910 shorter events, 880.4 us)
Async XLA Ops:
  7.2 55.3 %all-gather.11.cloned.1.call-start = ((), (), s32[]{:S(2)}) async-start(), calls=%async_computation.5 | async-start | bytes 2228224 | tf_op jit(solution)/shard_map/all_gather | solution.py:92
  7.2 6.4 collective-permute-start
  15.1 259.7 %all-gather.13.cloned.1.call-start = ((), (), s32[]{:S(2)}) async-start(), calls=%async_computation.6 | async-start | bytes 2228224 | tf_op jit(solution)/shard_map/all_gather | solution.py:92
  32.0 178.2 %copy-start.87 = (s32[1024]{0:T(1024)}, s32[1024]{0:T(1024)S(1)}, u32[]{:S(2)}) copy-start(s32[1024]{0:T(1024)S(1)} %pad_clamp_fusion.25) | copy-start | bytes 12292
  32.0 34.7 %copy-start.136 = (s32[1024]{0:T(1024)}, s32[1024]{0:T(1024)S(1)}, u32[]{:S(2)}) copy-start(s32[1024]{0:T(1024)S(1)} %pad_clamp_fusion.30) | copy-start | bytes 12292
  34.1 33.3 %copy-start.186 = (pred[64]{0:T(512)(128)(4,1)}, pred[64]{0:T(512)(128)(4,1)S(1)}, u32[]{:S(2)}) copy-start(pred[64]{0:T(512)(128)(4,1)S(1)} %get-tuple-element.163) | copy-start | bytes 196
  153.4 69.8 %copy-start.25 = (f32[256,256]{1,0:T(8,128)}, f32[256,256]{1,0:T(8,128)S(1)}, u32[]{:S(2)}) copy-start(f32[256,256]{1,0:T(8,128)S(1)} %select_maximum_fusion.9) | copy-start | bytes 786436
  154.9 54.8 %copy-start.24 = (f32[256,64]{1,0:T(8,128)S(1)}, f32[256,64]{1,0:T(8,128)}, u32[]{:S(2)}) copy-start(f32[256,64]{1,0:T(8,128)} %gather_fusion.33) | copy-start | bytes 196612
  162.6 47.3 %copy-start = (f32[256,512]{1,0:T(8,128)S(1)}, f32[256,512]{1,0:T(8,128)}, u32[]{:S(2)}) copy-start(f32[256,512]{1,0:T(8,128)} %gather_fusion.40) | copy-start | bytes 1572868
  162.6 47.3 %copy-start.209 = (pred[256]{0:T(512)(128)(4,1)S(1)}, pred[256]{0:T(512)(128)(4,1)}, u32[]{:S(2)}) copy-start(pred[256]{0:T(512)(128)(4,1)} %get-tuple-element.143) | copy-start | bytes 772
  225.0 7.7 collective-permute-start.1
  233.4 252.0 %all-gather.15.cloned.1.call-start = ((), (), s32[]{:S(2)}) async-start(), calls=%async_computation.7 | async-start | bytes 2228224 | tf_op jit(solution)/shard_map/all_gather | solution.py:92
  250.0 26.5 %copy-start.127 = (s32[256]{0:T(256)}, s32[256]{0:T(256)S(1)}, u32[]{:S(2)}) copy-start(s32[256]{0:T(256)S(1)} %gather_fusion.19) | copy-start | bytes 3076
  365.3 69.9 %copy-start.29 = (f32[256,256]{1,0:T(8,128)}, f32[256,256]{1,0:T(8,128)S(1)}, u32[]{:S(2)}) copy-start(f32[256,256]{1,0:T(8,128)S(1)} %select_maximum_fusion.8) | copy-start | bytes 786436
  367.5 54.3 %copy-start.18 = (f32[256,64]{1,0:T(8,128)S(1)}, f32[256,64]{1,0:T(8,128)}, u32[]{:S(2)}) copy-start(f32[256,64]{1,0:T(8,128)} %gather_fusion.45) | copy-start | bytes 196612
  374.8 47.2 %copy-start.1 = (f32[256,512]{1,0:T(8,128)S(1)}, f32[256,512]{1,0:T(8,128)}, u32[]{:S(2)}) copy-start(f32[256,512]{1,0:T(8,128)} %gather_fusion.54) | copy-start | bytes 1572868
  374.8 47.2 %copy-start.207 = (pred[256]{0:T(512)(128)(4,1)S(1)}, pred[256]{0:T(512)(128)(4,1)}, u32[]{:S(2)}) copy-start(pred[256]{0:T(512)(128)(4,1)} %get-tuple-element.82) | copy-start | bytes 772
  398.6 23.6 %copy-start.97 = (s32[1024]{0:T(1024)S(1)}, s32[1024]{0:T(1024)}, u32[]{:S(2)}) copy-start(s32[1024]{0:T(1024)} %copy-done.95) | copy-start | bytes 12292
  437.1 6.2 collective-permute-start.2
  443.9 207.9 %collective-permute-start.5 = (f32[64,128]{1,0:T(8,128)}, f32[64,128]{1,0:T(8,128)}, u32[]{:S(2)}, u32[]{:S(2)}) collective-permute-start(f32[64,128]{1,0:T(8,128)} %bitcast.331), channel_id=1, source_target_pairs={{0,16},{16,0},{32,48},{48,32},{64,80},{80,64},{96,112},{112,96},{1... | collective-permute-start | bytes 98312 | tf_op jit(solution)/shard_map/ppermute | solution.py:14
  457.1 30.1 %copy-start.113 = (s32[512]{0:T(512)}, s32[512]{0:T(512)S(1)}, u32[]{:S(2)}) copy-start(s32[512]{0:T(512)S(1)} %gather_fusion.24) | copy-start | bytes 6148
  462.0 25.2 %copy-start.115 = (s32[512]{0:T(512)}, s32[512]{0:T(512)S(1)}, u32[]{:S(2)}) copy-start(s32[512]{0:T(512)S(1)} %gather_fusion.25) | copy-start | bytes 6148
  463.8 28.3 %copy-start.99 = (s32[1024]{0:T(1024)}, s32[1024]{0:T(1024)S(1)}, u32[]{:S(2)}) copy-start(s32[1024]{0:T(1024)S(1)} %pad_clamp_fusion.13) | copy-start | bytes 12292
  463.8 24.2 %copy-start.138 = (s32[1024]{0:T(1024)}, s32[1024]{0:T(1024)S(1)}, u32[]{:S(2)}) copy-start(s32[1024]{0:T(1024)S(1)} %pad_clamp_fusion.17) | copy-start | bytes 12292
  575.8 69.9 %copy-start.27 = (f32[256,256]{1,0:T(8,128)}, f32[256,256]{1,0:T(8,128)S(1)}, u32[]{:S(2)}) copy-start(f32[256,256]{1,0:T(8,128)S(1)} %select_maximum_fusion.7) | copy-start | bytes 786436
  578.0 54.2 %copy-start.19 = (f32[256,64]{1,0:T(8,128)S(1)}, f32[256,64]{1,0:T(8,128)}, u32[]{:S(2)}) copy-start(f32[256,64]{1,0:T(8,128)} %gather_fusion.59) | copy-start | bytes 196612
  585.2 47.1 %copy-start.2 = (f32[256,512]{1,0:T(8,128)S(1)}, f32[256,512]{1,0:T(8,128)}, u32[]{:S(2)}) copy-start(f32[256,512]{1,0:T(8,128)} %gather_fusion.68) | copy-start | bytes 1572868
  585.2 47.1 %copy-start.203 = (pred[256]{0:T(512)(128)(4,1)S(1)}, pred[256]{0:T(512)(128)(4,1)}, u32[]{:S(2)}) copy-start(pred[256]{0:T(512)(128)(4,1)} %get-tuple-element.145) | copy-start | bytes 772
  647.6 10.1 collective-permute-start.3
  653.5 21.8 %all-to-all-start = ((f32[8,2,64,128]{3,2,1,0:T(8,128)}), f32[8,2,64,128]{3,2,1,0:T(8,128)S(1)}, u32[]{:S(2)}, u32[]{:S(2)}) async-start(f32[8,2,64,128]{3,2,1,0:T(8,128)} %stack.155), calls=%async_computation | async-start | bytes 1048576 | tf_op jit(solution)/shard_map/all_to_all | solution.py:98
  657.6 68.7 %all-gather.17.cloned.1.call-start = ((), (), s32[]{:S(2)}) async-start(), calls=%async_computation.8 | async-start | bytes 2228224 | tf_op jit(solution)/shard_map/all_gather | solution.py:92
  668.3 61.4 %copy-start.196 = (pred[64]{0:T(512)(128)(4,1)}, pred[64]{0:T(512)(128)(4,1)S(1)}, u32[]{:S(2)}) copy-start(pred[64]{0:T(512)(128)(4,1)S(1)} %get-tuple-element.94) | copy-start | bytes 196
  681.1 7.3 collective-permute-start.6
  686.0 48.1 %copy-start.104 = (s32[1024]{0:T(1024)}, s32[1024]{0:T(1024)S(1)}, u32[]{:S(2)}) copy-start(s32[1024]{0:T(1024)S(1)} %pad_clamp_fusion.7) | copy-start | bytes 12292
  689.3 20.3 %all-to-all-start.1 = ((f32[8,2,64,128]{3,2,1,0:T(8,128)}), f32[8,2,64,128]{3,2,1,0:T(8,128)S(1)}, u32[]{:S(2)}, u32[]{:S(2)}) async-start(f32[8,2,64,128]{3,2,1,0:T(8,128)} %stack.159), calls=%async_computation.1 | async-start | bytes 1048576 | tf_op jit(solution)/shard_map/all_to_all | solution.py:98
  715.5 5.8 collective-permute-start.7
  722.2 178.5 %all-to-all-start.2 = ((f32[8,2,64,128]{3,2,1,0:T(8,128)}), f32[8,2,64,128]{3,2,1,0:T(8,128)}, u32[]{:S(2)}, u32[]{:S(2)}) async-start(f32[8,2,64,128]{3,2,1,0:T(8,128)} %stack.163), calls=%async_computation.2 | async-start | bytes 1048576 | tf_op jit(solution)/shard_map/all_to_all | solution.py:98
  726.3 252.9 %all-gather.19.cloned.1.call-start = ((), (), s32[]{:S(2)}) async-start(), calls=%async_computation.9 | async-start | bytes 2228224 | tf_op jit(solution)/shard_map/all_gather | solution.py:92
  826.6 48.2 %copy-start.3 = (f32[256,512]{1,0:T(8,128)S(1)}, f32[256,512]{1,0:T(8,128)}, u32[]{:S(2)}) copy-start(f32[256,512]{1,0:T(8,128)} %gather_fusion.82) | copy-start | bytes 1572868
  826.6 48.2 %copy-start.205 = (pred[256]{0:T(512)(128)(4,1)S(1)}, pred[256]{0:T(512)(128)(4,1)}, u32[]{:S(2)}) copy-start(pred[256]{0:T(512)(128)(4,1)} %get-tuple-element.74) | copy-start | bytes 772
  850.9 24.1 %copy-start.106 = (s32[1024]{0:T(1024)S(1)}, s32[1024]{0:T(1024)}, u32[]{:S(2)}) copy-start(s32[1024]{0:T(1024)} %copy-done.104) | copy-start | bytes 12292
  889.9 10.1 collective-permute-start.4
  907.1 6.7 collective-permute-start.8
  914.6 25.4 %all-to-all-start.3 = ((f32[8,2,64,128]{3,2,1,0:T(8,128)}), f32[8,2,64,128]{3,2,1,0:T(8,128)S(1)}, u32[]{:S(2)}, u32[]{:S(2)}) async-start(f32[8,2,64,128]{3,2,1,0:T(8,128)} %stack.167), calls=%async_computation.3 | async-start | bytes 1048576 | tf_op jit(solution)/shard_map/all_to_all | solution.py:98
  945.6 9.7 collective-permute-start.9
  956.2 17.4 %all-to-all-start.4 = ((f32[8,2,64,128]{3,2,1,0:T(8,128)}), f32[8,2,64,128]{3,2,1,0:T(8,128)S(1)}, u32[]{:S(2)}, u32[]{:S(2)}) async-start(f32[8,2,64,128]{3,2,1,0:T(8,128)} %stack.171), calls=%async_computation.4 | async-start | bytes 1048576 | tf_op jit(solution)/shard_map/all_to_all | solution.py:98
  1077.6 47.6 %copy-start.4 = (f32[256,512]{1,0:T(8,128)S(1)}, f32[256,512]{1,0:T(8,128)}, u32[]{:S(2)}) copy-start(f32[256,512]{1,0:T(8,128)} %gather_fusion.96) | copy-start | bytes 1572868
  1077.6 47.6 %copy-start.201 = (pred[256]{0:T(512)(128)(4,1)S(1)}, pred[256]{0:T(512)(128)(4,1)}, u32[]{:S(2)}) copy-start(pred[256]{0:T(512)(128)(4,1)} %get-tuple-element.147) | copy-start | bytes 772
  (227 other events, 1094.6 us)
Sparse Core Ops, SparseCore 0:
  15.2 47.2 all-gather.10
  233.5 41.2 all-gather.12
  444.0 41.2 all-gather.14
  660.3 44.5 all-gather.16
  900.7 47.7 all-gather.18
